TPU v7x, 32 devices: a whole 2x2x4 slice. The times are simulated.
32 devices in a mesh: group: 2 (over y), gx: 4 (over z), gy: 2 (over x), ta: 2 (over core).
Axes of the slice: x: 2, y: 2, z: 4, core: 2. Of those that a mesh axis runs over, the one named last changes fastest.
Arguments:
- velocity: float32 [8, 3, 16, 16, 512], P(('group', 'ta'), None, 'gx', 'gy'), parts along dimension 0, may hold values from -4 to 4
- moved_image: float32 [8, 16, 16, 512], P(('group', 'ta'), 'gx', 'gy'), parts along dimension 0, may hold values from -6 to 6
- residual_weight: float32 [8, 16, 16, 512], P(('group', 'ta'), 'gx', 'gy'), parts along dimension 0, may hold values from -6 to 6
- mark_values: bfloat16 [4096, 3, 512], P(('group', 'gx', 'gy', 'ta')), parts along dimension 0, may hold values from -6 to 6
- mark_brick: int32 [4096, 1], P(('group', 'gx', 'gy', 'ta')), parts along dimension 0, may hold values from 0 to 3; in each aligned block of 128 rows (0 to 127, 128 to 255, ...) at most 64 rows name the same one
- mark_cell: int32 [4096, 1], P(('group', 'gx', 'gy', 'ta')), parts along dimension 0, may hold values from 0 to 31
- band_widths: int32 [3], replicated, may hold values from 3 to 8
Outputs:
- gradient: float32 [8, 3, 16, 16, 512], P(('group', 'ta'), None, 'gx', 'gy'), parts along dimension 0
There are 2 independent parts, one for each index of `group`. A program takes and returns all parts, laid end to end along the dimension named above; an argument that names none is the same for every part. Nothing has to cross between parts.
Inputs may be any that keep to these rules, and one draw needn't show every extreme that they name: `mark_brick`: in the rows of one device no brick index appears more than 64 times.
All inputs are finite; a program needn't handle non-finite values.
Results may differ from a plain program's by a relative error of at most 0.0018.
Values may be sent and summed in bfloat16 or wider, within the bound.
A program may use at most 64 MiB of HBM per device.

v0:
```python
import jax
import jax.numpy as jnp
from jax import lax
from jax.sharding import PartitionSpec as P

BMAX = 8


def extended(shard, sides, width):
    for axis, dim in sides:
        size, length = (lax.axis_size(axis), shard.shape[dim])
        up = [(i, (i + 1) % size) for i in range(size - 1)]
        down = [(j, i) for i, j in up]
        last = lax.slice_in_dim(shard, length - width, length, axis=dim)
        initial = lax.slice_in_dim(shard, 0, width, axis=dim)
        before = lax.ppermute(last, axis, up)
        after = lax.ppermute(initial, axis, down)
        shard = jnp.concatenate([before, shard, after], axis=dim)
    return shard


def tent_weights(offsets, width):
    spread = jnp.abs(offsets).astype(jnp.float32)
    widthf = width.astype(jnp.float32)
    inside = jnp.where(
        jnp.abs(offsets) <= width, (widthf + 1.0 - spread) / ((widthf + 1.0) * (widthf + 1.0)), 0.0
    )
    return inside + jnp.where(offsets == 0, 0.5, 0.0).astype(jnp.float32)


def square_matrix(count, width):
    indices = jnp.arange(count, dtype=jnp.int32)
    return tent_weights(indices[:, None] - indices[None, :], width)


def shards(velocity, moved_image, residual_weight, mark_values, mark_brick, mark_cell, band_widths):
    high = lax.Precision.HIGHEST
    steps_t, cells_x, cells_y, cells_z = moved_image.shape
    padded = extended(moved_image.astype(jnp.bfloat16), (("gx", 1), ("gy", 2)), 1).astype(
        moved_image.dtype
    )
    slope_x = (padded[:, 2:, 1:-1] - padded[:, :-2, 1:-1]) * 0.5
    slope_y = (padded[:, 1:-1, 2:] - padded[:, 1:-1, :-2]) * 0.5
    zpadded = jnp.pad(moved_image, ((0, 0), (0, 0), (0, 0), (1, 1)))
    slope_z = (zpadded[..., 2:] - zpadded[..., :-2]) * 0.5
    force = residual_weight[:, None] * jnp.stack([slope_x, slope_y, slope_z], axis=1)
    rows = mark_values.shape[0]
    bricks_x = lax.axis_size("gx")
    capacity = max(2, 2 * rows // bricks_x)
    target = mark_brick[:, 0]
    member = (target[:, None] == jnp.arange(bricks_x, dtype=jnp.int32)[None, :]).astype(jnp.int32)
    before = jnp.cumsum(member, axis=0) - member
    position = jnp.sum(before * member, axis=1)
    slot_index = target * capacity + position
    placed = slot_index[:, None] == jnp.arange(bricks_x * capacity, dtype=jnp.int32)[None, :]
    per_time = rows // steps_t
    cell_index = (
        jnp.arange(rows, dtype=jnp.int32) // per_time * (cells_x * cells_y) + mark_cell[:, 0]
    )
    filled = jnp.sum(placed.astype(jnp.int32), axis=0)
    slot_cells = jnp.where(
        filled > 0, jnp.sum(jnp.where(placed, cell_index[:, None], 0), axis=0), -1
    )
    flat_values = mark_values.reshape(rows, 3 * cells_z)
    slot_values = jnp.dot(
        placed.T.astype(jnp.bfloat16), flat_values, preferred_element_type=jnp.float32
    ).astype(jnp.bfloat16)
    arrived_values, arrived_cells = (
        lax.all_to_all(
            slot_values.reshape(bricks_x, capacity, 3 * cells_z),
            "gx",
            split_axis=0,
            concat_axis=0,
            tiled=True,
        ),
        lax.all_to_all(
            slot_cells.reshape(bricks_x, capacity), "gx", split_axis=0, concat_axis=0, tiled=True
        ),
    )
    hits = (
        jnp.arange(steps_t * cells_x * cells_y, dtype=jnp.int32)[:, None]
        == arrived_cells.reshape(-1)[None, :]
    ).astype(jnp.bfloat16)
    landed = jnp.dot(
        hits,
        arrived_values.reshape(bricks_x * capacity, 3 * cells_z),
        preferred_element_type=jnp.float32,
    )
    landed = landed.reshape(steps_t, cells_x, cells_y, 3, cells_z).transpose(0, 3, 1, 2, 4)
    total = force + landed
    arrived = lax.all_to_all(total, "gx", split_axis=4, concat_axis=2, tiled=True)
    length = arrived.shape[2]
    flattened = arrived.reshape(arrived.shape[0], 3, length, -1)
    result = jnp.einsum(
        "ij,tcjr->tcir", square_matrix(length, band_widths[0]), flattened, precision=high
    )
    along_first = lax.all_to_all(
        result.reshape(arrived.shape), "gx", split_axis=2, concat_axis=4, tiled=True
    )
    widened = extended(along_first, (("gy", 3),), BMAX)
    rowids = jnp.arange(cells_y, dtype=jnp.int32)
    colids = jnp.arange(cells_y + 2 * BMAX, dtype=jnp.int32) - BMAX
    matrix = tent_weights(rowids[:, None] - colids[None, :], band_widths[1])
    along_second = jnp.einsum("ij,tcxjz->tcxiz", matrix, widened, precision=high)
    smoothed = jnp.einsum(
        "tcxyj,ij->tcxyi", along_second, square_matrix(cells_z, band_widths[2]), precision=high
    )
    return velocity - smoothed


def solution(mesh):
    return jax.shard_map(
        shards,
        mesh=mesh,
        in_specs=(
            P(("group", "ta"), None, "gx", "gy", None),
            P(("group", "ta"), "gx", "gy", None),
            P(("group", "ta"), "gx", "gy", None),
            P(("group", "gx", "gy", "ta"), None, None),
            P(("group", "gx", "gy", "ta"), None),
            P(("group", "gx", "gy", "ta"), None),
            P(),
        ),
        out_specs=P(("group", "ta"), None, "gx", "gy", None),
        check_vma=False,
    )
```

profile of v0, /device:TPU:0, one launch (start us, length us, event | category | flops | bytes accessed | tf_op | source)
XLA Modules:
  0.0 124.1 jit_solution(996437194319154870)
XLA Ops:
  0.0 0.7 fusion.35
  0.7 0.2 reduce_window_sum.11
  0.9 0.8 select_reduce_fusion.1
  1.7 0.7 fusion.82
  2.4 0.1 convert_reduce_fusion
  2.6 0.7 select_n.58
  3.2 6.3 %all-to-all-start = ((s32[4,1,64]{2,1,0:T(1,128)}), s32[4,1,64]{2,1,0:T(1,128)S(1)}, u32[]{:S(2)}, u32[]{:S(2)}) async-start(s32[4,1,64]{2,1,0:T(1,128)} %select_n.58), calls=%async_computation | async-start | bytes 4096 | tf_op jit(solution)/shard_map/all_to_all | solution.py:76
  9.5 1.2 copy.43
  10.8 0.0 copy-start.1
  10.8 1.4 %convolution_convert_fusion = bf16[256,1536]{1,0:T(8,128)(2,1)} fusion(bf16[128,1536]{0,1:T(8,128)(2,1)S(1)} %bitcast.91, s32[128]{0:T(128)S(1)} %get-tuple-element.19), kind=kOutput, calls=%fused_computation | convolution fusion | flops 101122048 | bytes 1180160 | tf_op jit(solution)/shard_map/dot_general | solution.py:65
  12.1 2.9 %all-to-all-done = s32[4,1,64]{2,1,0:T(1,128)S(1)} async-done(((s32[4,1,64]{2,1,0:T(1,128)}), s32[4,1,64]{2,1,0:T(1,128)S(1)}, u32[]{:S(2)}, u32[]{:S(2)}) %all-to-all-start) | async-done | bytes 1056 | tf_op jit(solution)/shard_map/all_to_all | solution.py:76
  15.0 3.5 %all-to-all-start.1 = ((bf16[4,64,1536]{2,1,0:T(8,128)(2,1)}), bf16[4,64,1536]{2,1,0:T(8,128)(2,1)S(1)}, u32[]{:S(2)}, u32[]{:S(2)}) async-start(bf16[4,64,1536]{2,1,0:T(8,128)(2,1)} %bitcast.12), calls=%async_computation.1 | async-start | bytes 1572864 | tf_op jit(solution)/shard_map/all_to_all | solution.py:69
  18.5 0.0 copy-done.1
  18.5 0.1 fusion.94
  18.7 3.9 %collective-permute-start = (bf16[2,1,8,512]{3,2,1,0:T(8,128)(2,1)S(1)}, bf16[2,1,8,512]{3,2,1,0:T(8,128)(2,1)S(1)}, u32[]{:S(2)}, u32[]{:S(2)}) collective-permute-start(bf16[2,1,8,512]{3,2,1,0:T(8,128)(2,1)S(1)} %get-tuple-element.13), channel_id=1, source_target_pairs={{0,4},{4,8},{8,12},{1,5},{5,9},{9,13},{2,6},{6,10},{10,14},{3,7},{... | collective-permute-start | bytes 49160 | tf_op jit(solution)/shard_map/ppermute | solution.py:16
  22.6 1.3 %collective-permute-start.1 = (bf16[2,1,8,512]{3,2,1,0:T(8,128)(2,1)S(1)}, bf16[2,1,8,512]{3,2,1,0:T(8,128)(2,1)S(1)}, u32[]{:S(2)}, u32[]{:S(2)}) collective-permute-start(bf16[2,1,8,512]{3,2,1,0:T(8,128)(2,1)S(1)} %get-tuple-element.14), channel_id=1, source_target_pairs={{4,0},{8,4},{12,8},{5,1},{9,5},{13,9},{6,2},{10,6},{14,10},{7,3},{... | collective-permute-start | bytes 49160 | tf_op jit(solution)/shard_map/ppermute | solution.py:17
  23.9 6.6 %collective-permute-done = bf16[2,1,8,512]{3,2,1,0:T(8,128)(2,1)S(1)} collective-permute-done((bf16[2,1,8,512]{3,2,1,0:T(8,128)(2,1)S(1)}, bf16[2,1,8,512]{3,2,1,0:T(8,128)(2,1)S(1)}, u32[]{:S(2)}, u32[]{:S(2)}) %collective-permute-start) | collective-permute-done | bytes 16416 | tf_op jit(solution)/shard_map/ppermute | solution.py:16
  30.5 0.0 collective-permute-done.1
  30.5 3.4 %collective-permute-start.2 = (bf16[2,6,1,512]{3,2,1,0:T(2,128)(2,1)S(1)}, bf16[2,6,1,512]{3,2,1,0:T(2,128)(2,1)S(1)}, u32[]{:S(2)}, u32[]{:S(2)}) collective-permute-start(bf16[2,6,1,512]{3,2,1,0:T(2,128)(2,1)S(1)} %get-tuple-element.11), channel_id=1, source_target_pairs={{0,2},{1,3},{4,6},{5,7},{8,10},{9,11},{12,14},{13,15},{16,18},{17,... | collective-permute-start | bytes 36872 | tf_op jit(solution)/shard_map/ppermute | solution.py:16
  33.9 1.3 %collective-permute-start.3 = (bf16[2,6,1,512]{3,2,1,0:T(2,128)(2,1)S(1)}, bf16[2,6,1,512]{3,2,1,0:T(2,128)(2,1)S(1)}, u32[]{:S(2)}, u32[]{:S(2)}) collective-permute-start(bf16[2,6,1,512]{3,2,1,0:T(2,128)(2,1)S(1)} %get-tuple-element.12), channel_id=1, source_target_pairs={{2,0},{3,1},{6,4},{7,5},{10,8},{11,9},{14,12},{15,13},{18,16},{19,... | collective-permute-start | bytes 36872 | tf_op jit(solution)/shard_map/ppermute | solution.py:17
  35.2 0.5 broadcast.122
  35.8 0.7 reduce.3
  36.4 0.1 eq.95
  36.5 0.0 collective-permute-done.2
  36.5 3.1 %collective-permute-done.3 = bf16[2,6,1,512]{3,2,1,0:T(2,128)(2,1)S(1)} collective-permute-done((bf16[2,6,1,512]{3,2,1,0:T(2,128)(2,1)S(1)}, bf16[2,6,1,512]{3,2,1,0:T(2,128)(2,1)S(1)}, u32[]{:S(2)}, u32[]{:S(2)}) %collective-permute-start.3) | collective-permute-done | bytes 12320 | tf_op jit(solution)/shard_map/ppermute | solution.py:17
  39.7 0.1 maximum_convert_fusion
  39.7 0.0 copy-start
  39.8 0.0 all-to-all-done.1
  39.8 0.3 copy.44
  40.1 0.6 copy-done
  40.7 0.4 fusion
  41.0 4.6 %copy.45 = f32[2,3,4,8,512]{3,2,1,0,4:T(4,128)} copy(f32[2,3,4,8,512]{4,3,1,2,0:T(8,128)S(1)} %fusion) | data formatting | bytes 786432 | tf_op jit(solution)/shard_map/add | solution.py:90
  45.6 0.0 copy-start.2
  45.6 9.2 %reshape.133 = f32[4,1,24576]{2,1,0:T(1,128)} reshape(f32[512,2,3,4,8]{4,3,2,1,0:T(4,128)} %bitcast.80) | data formatting | bytes 786432
  54.9 9.1 %all-to-all-start.2 = ((f32[4,1,24576]{2,1,0:T(1,128)}), f32[4,1,24576]{2,1,0:T(1,128)S(1)}, u32[]{:S(2)}, u32[]{:S(2)}) async-start(f32[4,1,24576]{2,1,0:T(1,128)} %reshape.133), calls=%async_computation.2 | async-start | bytes 786432 | tf_op jit(solution)/shard_map/all_to_all | solution.py:91
  64.0 0.0 copy-done.2
  64.0 0.6 fusion.96
  65.3 7.9 %all-to-all-done.2 = f32[4,1,24576]{2,1,0:T(1,128)S(1)} async-done(((f32[4,1,24576]{2,1,0:T(1,128)}), f32[4,1,24576]{2,1,0:T(1,128)S(1)}, u32[]{:S(2)}, u32[]{:S(2)}) %all-to-all-start.2) | async-done | bytes 393248 | tf_op jit(solution)/shard_map/all_to_all | solution.py:91
  73.2 0.5 broadcast.123
  73.7 1.8 %reduce.4 = f32[4,24576]{1,0:T(4,128)S(1)} reduce(f32[4,1,24576]{2,1,0:T(1,128)S(1)} %all-to-all-done.2, f32[]{:T(128)} %broadcast.123), dimensions={1}, to_apply=%all_to_all.33.reduce_sub_computation | reduce | bytes 786436 | tf_op jit(solution)/shard_map/all_to_all | solution.py:91
  75.4 10.3 %reshape.134 = f32[512,2,3,4,8]{4,3,2,1,0:T(4,128)} reshape(f32[4,24576]{1,0:T(4,128)S(1)} %reduce.4) | data formatting | bytes 786432
  85.7 5.0 %copy.46 = f32[2,3,4,8,4,128]{5,3,2,4,1,0:T(8,128)S(1)} copy(f32[2,3,4,8,4,128]{3,2,1,0,5,4:T(4,128)} %bitcast.81) | data formatting | bytes 786432 | tf_op jit(solution)/shard_map/all_to_all | solution.py:91
  90.7 0.1 reshape.117
  90.8 1.1 fusion.40
  91.9 0.1 copy.56
  92.0 13.6 %all_to_all.44 = f32[2,3,16,8,128]{4,3,1,0,2:T(8,128)S(1)} all-to-all(f32[2,3,16,8,128]{4,3,1,0,2:T(8,128)S(1)} %copy.47), channel_id=1, replica_groups=mesh['group'=2,'gx'=4,'gy'=2,'ta'=2] {'gx'}, dimensions={2} | all-to-all | bytes 786432 | tf_op jit(solution)/shard_map/all_to_all | solution.py:97
  105.6 0.0 copy-start.3
  105.7 3.4 %collective-permute-start.4 = (f32[2,3,4,8,512]{4,3,2,1,0:T(8,128)S(1)}, f32[2,3,4,8,512]{4,3,2,1,0:T(8,128)S(1)}, u32[]{:S(2)}, u32[]{:S(2)}) collective-permute-start(f32[2,3,4,8,512]{4,3,2,1,0:T(8,128)S(1)} %bitcast.87), channel_id=1, source_target_pairs={{0,2},{1,3},{4,6},{5,7},{8,10},{9,11},{12,14},{13,15},{16,18},{17,... | collective-permute-start | bytes 1179656 | tf_op jit(solution)/shard_map/ppermute | solution.py:16
  109.0 1.3 %collective-permute-start.5 = (f32[2,3,4,8,512]{4,3,2,1,0:T(8,128)S(1)}, f32[2,3,4,8,512]{4,3,2,1,0:T(8,128)S(1)}, u32[]{:S(2)}, u32[]{:S(2)}) collective-permute-start(f32[2,3,4,8,512]{4,3,2,1,0:T(8,128)S(1)} %bitcast.88), channel_id=1, source_target_pairs={{2,0},{3,1},{6,4},{7,5},{10,8},{11,9},{14,12},{15,13},{18,16},{19,... | collective-permute-start | bytes 1179656 | tf_op jit(solution)/shard_map/ppermute | solution.py:17
  111.5 4.3 %collective-permute-done.4 = f32[2,3,4,8,512]{4,3,2,1,0:T(8,128)S(1)} collective-permute-done((f32[2,3,4,8,512]{4,3,2,1,0:T(8,128)S(1)}, f32[2,3,4,8,512]{4,3,2,1,0:T(8,128)S(1)}, u32[]{:S(2)}, u32[]{:S(2)}) %collective-permute-start.4) | collective-permute-done | bytes 393248 | tf_op jit(solution)/shard_map/ppermute | solution.py:16
  115.8 4.1 %collective-permute-done.5 = f32[2,3,4,8,512]{4,3,2,1,0:T(8,128)S(1)} collective-permute-done((f32[2,3,4,8,512]{4,3,2,1,0:T(8,128)S(1)}, f32[2,3,4,8,512]{4,3,2,1,0:T(8,128)S(1)}, u32[]{:S(2)}, u32[]{:S(2)}) %collective-permute-start.5) | collective-permute-done | bytes 393248 | tf_op jit(solution)/shard_map/ppermute | solution.py:17
  119.9 1.3 %convolution_bitcast_fusion = f32[2,3,4,8,512]{4,3,2,1,0:T(8,128)S(1)} fusion(f32[2,3,4,8,512]{4,3,2,1,0:T(8,128)S(1)} %collective-permute-done.5, f32[2,3,4,8,512]{4,3,2,1,0:T(8,128)S(1)} %bitcast.89, f32[2,3,4,8,512]{4,3,2,1,0:T(8,128)S(1)} %collective-permute-done.4, f32[]{:T(128)S(6)} %mul.60, f32[]{:T(128)S(6)} %add.63, s32[]{:T(128)} %bitcast.29, ...), kind=kOutput, calls=%fused_computation.2 | convolution fusion | flops 28903296 | bytes 1572972 | tf_op jit(solution)/shard_map/ij,tcxjz->tcxiz/dot_general | solution.py:104
  121.3 0.0 copy-done.3
  121.3 2.8 %convolution_subtract_fusion = f32[2,3,4,8,512]{4,3,2,1,0:T(8,128)} fusion(f32[2,3,4,8,512]{4,3,2,1,0:T(8,128)S(1)} %copy-done.3, f32[2,3,4,8,512]{4,3,2,1,0:T(8,128)S(1)} %convolution_bitcast_fusion, f32[]{:T(128)S(6)} %mul.61, f32[]{:T(128)S(6)} %add.65, s32[]{:T(128)} %bitcast.33), kind=kOutput, calls=%fused_computation.1 | convolution fusion | flops 606699520 | bytes 1179660 | tf_op jit(solution)/shard_map/tcxyj,ij->tcxyi/dot_general | solution.py:105
  (8 shorter events, 0.2 us)
Async XLA Ops:
  3.2 11.8 %all-to-all-start = ((s32[4,1,64]{2,1,0:T(1,128)}), s32[4,1,64]{2,1,0:T(1,128)S(1)}, u32[]{:S(2)}, u32[]{:S(2)}) async-start(s32[4,1,64]{2,1,0:T(1,128)} %select_n.58), calls=%async_computation | async-start | bytes 4096 | tf_op jit(solution)/shard_map/all_to_all | solution.py:76
  10.8 7.8 %copy-start.1 = (f32[2,4,8,512]{3,2,1,0:T(8,128)S(1)}, f32[2,4,8,512]{3,2,1,0:T(8,128)}, u32[]{:S(2)}) copy-start(f32[2,4,8,512]{3,2,1,0:T(8,128)} %param.8) | copy-start | bytes 393220
  15.0 24.8 %all-to-all-start.1 = ((bf16[4,64,1536]{2,1,0:T(8,128)(2,1)}), bf16[4,64,1536]{2,1,0:T(8,128)(2,1)S(1)}, u32[]{:S(2)}, u32[]{:S(2)}) async-start(bf16[4,64,1536]{2,1,0:T(8,128)(2,1)} %bitcast.12), calls=%async_computation.1 | async-start | bytes 1572864 | tf_op jit(solution)/shard_map/all_to_all | solution.py:69
  18.7 11.8 %collective-permute-start = (bf16[2,1,8,512]{3,2,1,0:T(8,128)(2,1)S(1)}, bf16[2,1,8,512]{3,2,1,0:T(8,128)(2,1)S(1)}, u32[]{:S(2)}, u32[]{:S(2)}) collective-permute-start(bf16[2,1,8,512]{3,2,1,0:T(8,128)(2,1)S(1)} %get-tuple-element.13), channel_id=1, source_target_pairs={{0,4},{4,8},{8,12},{1,5},{5,9},{9,13},{2,6},{6,10},{10,14},{3,7},{... | collective-permute-start | bytes 49160 | tf_op jit(solution)/shard_map/ppermute | solution.py:16
  22.6 7.9 %collective-permute-start.1 = (bf16[2,1,8,512]{3,2,1,0:T(8,128)(2,1)S(1)}, bf16[2,1,8,512]{3,2,1,0:T(8,128)(2,1)S(1)}, u32[]{:S(2)}, u32[]{:S(2)}) collective-permute-start(bf16[2,1,8,512]{3,2,1,0:T(8,128)(2,1)S(1)} %get-tuple-element.14), channel_id=1, source_target_pairs={{4,0},{8,4},{12,8},{5,1},{9,5},{13,9},{6,2},{10,6},{14,10},{7,3},{... | collective-permute-start | bytes 49160 | tf_op jit(solution)/shard_map/ppermute | solution.py:17
  30.5 6.0 %collective-permute-start.2 = (bf16[2,6,1,512]{3,2,1,0:T(2,128)(2,1)S(1)}, bf16[2,6,1,512]{3,2,1,0:T(2,128)(2,1)S(1)}, u32[]{:S(2)}, u32[]{:S(2)}) collective-permute-start(bf16[2,6,1,512]{3,2,1,0:T(2,128)(2,1)S(1)} %get-tuple-element.11), channel_id=1, source_target_pairs={{0,2},{1,3},{4,6},{5,7},{8,10},{9,11},{12,14},{13,15},{16,18},{17,... | collective-permute-start | bytes 36872 | tf_op jit(solution)/shard_map/ppermute | solution.py:16
  33.9 5.7 %collective-permute-start.3 = (bf16[2,6,1,512]{3,2,1,0:T(2,128)(2,1)S(1)}, bf16[2,6,1,512]{3,2,1,0:T(2,128)(2,1)S(1)}, u32[]{:S(2)}, u32[]{:S(2)}) collective-permute-start(bf16[2,6,1,512]{3,2,1,0:T(2,128)(2,1)S(1)} %get-tuple-element.12), channel_id=1, source_target_pairs={{2,0},{3,1},{6,4},{7,5},{10,8},{11,9},{14,12},{15,13},{18,16},{19,... | collective-permute-start | bytes 36872 | tf_op jit(solution)/shard_map/ppermute | solution.py:17
  39.7 0.9 copy-start
  45.6 18.4 %copy-start.2 = (s32[3]{0:T(128)S(1)}, s32[3]{0:T(128)}, u32[]{:S(2)}) copy-start(s32[3]{0:T(128)} %param.13) | copy-start | bytes 40
  54.9 18.3 %all-to-all-start.2 = ((f32[4,1,24576]{2,1,0:T(1,128)}), f32[4,1,24576]{2,1,0:T(1,128)S(1)}, u32[]{:S(2)}, u32[]{:S(2)}) async-start(f32[4,1,24576]{2,1,0:T(1,128)} %reshape.133), calls=%async_computation.2 | async-start | bytes 786432 | tf_op jit(solution)/shard_map/all_to_all | solution.py:91
  105.6 15.7 %copy-start.3 = (f32[2,3,4,8,512]{4,3,2,1,0:T(8,128)S(1)}, f32[2,3,4,8,512]{4,3,2,1,0:T(8,128)}, u32[]{:S(2)}) copy-start(f32[2,3,4,8,512]{4,3,2,1,0:T(8,128)} %param.7) | copy-start | bytes 1179652
  105.7 10.2 %collective-permute-start.4 = (f32[2,3,4,8,512]{4,3,2,1,0:T(8,128)S(1)}, f32[2,3,4,8,512]{4,3,2,1,0:T(8,128)S(1)}, u32[]{:S(2)}, u32[]{:S(2)}) collective-permute-start(f32[2,3,4,8,512]{4,3,2,1,0:T(8,128)S(1)} %bitcast.87), channel_id=1, source_target_pairs={{0,2},{1,3},{4,6},{5,7},{8,10},{9,11},{12,14},{13,15},{16,18},{17,... | collective-permute-start | bytes 1179656 | tf_op jit(solution)/shard_map/ppermute | solution.py:16
  109.0 10.9 %collective-permute-start.5 = (f32[2,3,4,8,512]{4,3,2,1,0:T(8,128)S(1)}, f32[2,3,4,8,512]{4,3,2,1,0:T(8,128)S(1)}, u32[]{:S(2)}, u32[]{:S(2)}) collective-permute-start(f32[2,3,4,8,512]{4,3,2,1,0:T(8,128)S(1)} %bitcast.88), channel_id=1, source_target_pairs={{2,0},{3,1},{6,4},{7,5},{10,8},{11,9},{14,12},{15,13},{18,16},{19,... | collective-permute-start | bytes 1179656 | tf_op jit(solution)/shard_map/ppermute | solution.py:17
where the time goes:
time: 125 us; the launch traced here: 124 us
  local copies, waits for them, and re-layouts  33.8 us (27%)
  starting transfers between devices  33.5 us (27%)
  waiting for transfers between devices  28.9 us (23%)
  blocking collectives  13.6 us (11%)
  matrix products  6.99 us (6%)
  other arithmetic  5.27 us (4%)
  between operations  2.04 us (2%)
    unnamed x12, local copies, waits for them, and re-layouts  21.3 us
    all_to_all x1, blocking collectives, shards(): lax.all_to_all(result.reshape(arrived.shape), 'gx', split_axis=2, concat_...  13.6 us
    ppermute x3, waiting for transfers between devices, extended(): before = lax.ppermute(last, axis, up)  10.9 us
    ppermute x3, starting transfers between devices, extended(): before = lax.ppermute(last, axis, up)  10.7 us
    all_to_all x1, starting transfers between devices, shards(): lax.all_to_all(total, 'gx', split_axis=4, concat_axis=2, tiled=True)  9.13 us
    all_to_all x1, waiting for transfers between devices, shards(): lax.all_to_all(total, 'gx', split_axis=4, concat_axis=2, tiled=True)  7.87 us
    ppermute x3, waiting for transfers between devices, extended(): after = lax.ppermute(initial, axis, down)  7.28 us
    all_to_all x1, starting transfers between devices, shards(): lax.all_to_all(slot_cells.reshape(bricks_x, capacity), 'gx', split_axis=0...  6.32 us
  transfers between devices with their start and end apart: 9, of which 6 were waited for; matrix products, arithmetic and copies ran while one was open for 4% of the time, Pallas kernels for 0%

commit v1 on v0

v1 whole, which is shorter than its diff:
```python
import functools
import math

import jax
import jax.numpy as jnp
from jax import lax
from jax.experimental import pallas as pl
from jax.experimental.pallas import tpu as pltpu
from jax.sharding import PartitionSpec as P

LEVELS = 32000.0
MESH = pl.DeviceIdType.MESH


def each(start, stop, body):
    if stop - start <= 4:
        for i in range(start, stop):
            body(i)
    else:
        lax.fori_loop(start, stop, lambda i, c: (body(i), c)[1], 0)


def halves(x):
    hi = x.astype(jnp.bfloat16)
    return hi, (x - hi.astype(jnp.float32)).astype(jnp.bfloat16)


def tent(offsets, width):
    w1 = (width + 1).astype(jnp.float32)
    far = jnp.abs(offsets)
    inside = jnp.where(far <= width, (w1 - far.astype(jnp.float32)) / (w1 * w1), 0.0)
    return inside + jnp.where(offsets == 0, 0.5, 0.0)


def kernel(
    n_gx, n_gy, dims, width_ref, image_ref, weight_ref, mark_ref, brick_ref, cell_ref, out_ref,
    tx, scale_out, own, rx, scale_in, ytx, yown, yrx, edge_x, edge_y_out, edge_y, kmat, tmat,
    tx_send, rx_recv, s_send, s_recv, y_send, y_recv, ex_send, ex_recv, ey_send, ey_recv,
):
    steps, cx, cy, nz, rows = dims
    cells = cx * cy
    per = rows // steps
    lines = 2 * cells + per
    gx, gy = lax.axis_index("gx"), lax.axis_index("gy")
    left, right = gx > 0, gx < n_gx - 1
    low, high = gy > 0, gy < n_gy - 1
    barrier = pltpu.get_barrier_semaphore()

    def greet(s):
        pl.semaphore_signal(
            barrier, inc=1, device_id={"gx": lax.rem(gx + s, n_gx)}, device_id_type=MESH
        )

    each(1, n_gx, greet)

    @pl.when(low)
    def _():
        pl.semaphore_signal(barrier, inc=1, device_id={"gy": gy - 1}, device_id_type=MESH)

    @pl.when(high)
    def _():
        pl.semaphore_signal(barrier, inc=1, device_id={"gy": gy + 1}, device_id_type=MESH)

    for t in range(steps):
        for x in range(cx):
            r = t * cx + x
            edge_y_out[0, r : r + 1, :] = image_ref[t, x, 0:1, :]
            edge_y_out[1, r : r + 1, :] = image_ref[t, x, cy - 1 : cy, :]

    group = math.gcd(n_gx, 4)
    block = group * cells
    lane = lax.broadcasted_iota(jnp.int32, (1, lines), 1)
    fcell = lane & (cells - 1)
    for t in range(steps):
        is_mark = (lane >= t * per) & (lane < (t + 1) * per)
        sx = jnp.where(is_mark, brick_ref[...] * cx + cell_ref[...] // cy, gx * cx + fcell // cy)
        sy = jnp.where(is_mark, cell_ref[...] & (cy - 1), fcell & (cy - 1))

        def build(g, t=t, sx=sx, sy=sy):
            r = lax.broadcasted_iota(jnp.int32, (block, lines), 0)
            brick = gx + g * group + r // cells
            brick = jnp.where(brick >= n_gx, brick - n_gx, brick)
            x = brick * cx + (r // cy & (cx - 1))
            k = jnp.where((r & (cy - 1)) == sy, tent(x - sx, width_ref[0]), 0.0)
            hi, lo = halves(k)
            at = pl.ds(pl.multiple_of(g * block, block), block)
            kmat[t, at, 0:lines] = hi
            kmat[t, at, lines : 2 * lines] = lo

        each(0, n_gx // group, build)

    pl.semaphore_wait(barrier, n_gx - 1 + low.astype(jnp.int32) + high.astype(jnp.int32))

    def x_edge(d, plane, to):
        return pltpu.make_async_remote_copy(
            image_ref.at[:, plane], edge_x.at[d], ex_send.at[d], ex_recv.at[d],
            device_id={"gx": to}, device_id_type=MESH,
        )

    def y_edge(d, side, to):
        return pltpu.make_async_remote_copy(
            edge_y_out.at[side], edge_y.at[d], ey_send.at[d], ey_recv.at[d],
            device_id={"gy": to}, device_id_type=MESH,
        )

    exchanges = (
        (right, left, x_edge(0, cx - 1, gx + 1), edge_x, 0),
        (left, right, x_edge(1, 0, gx - 1), edge_x, 1),
        (high, low, y_edge(0, 1, gy + 1), edge_y, 0),
        (low, high, y_edge(1, 0, gy - 1), edge_y, 1),
    )
    for sends, receives, copy, buffer, d in exchanges:
        pl.when(sends)(copy.start)

        @pl.when(jnp.logical_not(receives))
        def _(buffer=buffer, d=d):
            buffer[d] = jnp.zeros(buffer.shape[1:], buffer.dtype)

    def brick_copy(k, s):
        return pltpu.make_async_remote_copy(
            tx.at[k, s], rx.at[k, s], tx_send.at[k, s], rx_recv.at[k, s],
            device_id={"gx": lax.rem(gx + s, n_gx)}, device_id_type=MESH,
        )

    def scale_copy(k, s):
        return pltpu.make_async_remote_copy(
            scale_out.at[k, s], scale_in.at[k, s], s_send.at[k, s], s_recv.at[k, s],
            device_id={"gx": lax.rem(gx + s, n_gx)}, device_id_type=MESH,
        )

    def send(k, s):
        brick_copy(k, s).start()
        scale_copy(k, s).start()

    def receive(k, s):
        brick_copy(k, s).wait_recv()
        scale_copy(k, s).wait_recv()
        return rx[k, s].astype(jnp.int32).astype(jnp.float32) * scale_in[k, s]

    def settle(k, s):
        brick_copy(k, s).wait_send()
        scale_copy(k, s).wait_send()

    order = [(t, c) for c in (2, 0, 1) for t in range(steps)]
    for k, (t, c) in enumerate(order):
        if k == steps:
            for _, receives, copy, _, _ in exchanges:
                pl.when(receives)(copy.wait_recv)
        m = image_ref[t]
        if c == 2:
            flat = m.reshape(cells, nz)
            z = lax.broadcasted_iota(jnp.int32, (cells, nz), 1)
            after = jnp.where(z == nz - 1, 0.0, pltpu.roll(flat, nz - 1, 1))
            before = jnp.where(z == 0, 0.0, pltpu.roll(flat, 1, 1))
            slope = after - before
        elif c == 0:
            after = jnp.concatenate([m[1:], edge_x[1, t][None]], axis=0)
            before = jnp.concatenate([edge_x[0, t][None], m[:-1]], axis=0)
            slope = (after - before).reshape(cells, nz)
        else:
            flat = m.reshape(cells, nz)
            y = lax.broadcasted_iota(jnp.int32, (cy, nz), 0)
            parts = []
            for x in range(cx):
                r = t * cx + x
                after = jnp.where(y == cy - 1, edge_y[1, r : r + 1, :], pltpu.roll(m[x], cy - 1, 0))
                before = jnp.where(y == 0, edge_y[0, r : r + 1, :], pltpu.roll(m[x], 1, 0))
                parts.append(after - before)
            slope = jnp.concatenate(parts, axis=0)
        hi, lo = halves(weight_ref[t].reshape(cells, nz) * slope * 0.5)
        marks = mark_ref[c, t * per : (t + 1) * per, :]
        pieces = [hi, lo]
        pieces.insert(0 if t == 0 else 2, marks)
        b = jnp.concatenate(pieces, axis=0)
        b = jnp.concatenate([b, b], axis=0)

        def spread(g, k=k, t=t, b=b):
            at = pl.ds(pl.multiple_of(g * block, block), block)
            p = jnp.dot(kmat[t, at, :], b, preferred_element_type=jnp.float32)
            for i in range(group):
                piece = p[i * cells : (i + 1) * cells]
                s = g * group + i
                top = jnp.maximum(jnp.max(jnp.abs(piece), axis=0, keepdims=True), 1e-30)
                tx[k, s] = jnp.round(piece * (LEVELS / top)).astype(jnp.int32).astype(jnp.int16)
                scale_out[k, s] = top * (1.0 / LEVELS)
                if i == 0:
                    if n_gx == group:
                        own[k] = piece
                    else:

                        @pl.when(g == 0)
                        def _():
                            own[k] = piece

        each(0, n_gx // group, spread)
        each(1, n_gx, lambda s, k=k: send(k, s))

    zi = lax.broadcasted_iota(jnp.int32, (nz, nz), 0)
    zj = lax.broadcasted_iota(jnp.int32, (nz, nz), 1)
    tmat[...] = (
        jnp.maximum(width_ref[2] + 1 - jnp.abs(zi - zj), 0).astype(jnp.float32).astype(jnp.bfloat16)
    )
    wz = jnp.full((1, nz), (width_ref[2] + 1).astype(jnp.float32), jnp.float32)
    inv = 1.0 / (wz * wz)

    r = lax.broadcasted_iota(jnp.int32, (3 * cells, cells), 0)
    q = lax.broadcasted_iota(jnp.int32, (3 * cells, cells), 1)
    which = r // cells
    shift = jnp.where(which == 1, cy, jnp.where(which == 2, -cy, 0))
    same = (r // cy & (cx - 1)) == q // cy
    ymat = jnp.where(same, tent((r & (cy - 1)) + shift - (q & (cy - 1)), width_ref[1]), 0.0)
    yhi, ylo = halves(ymat)
    ymats = jnp.concatenate([yhi, yhi, ylo], axis=1)

    def y_copy(k, d, to):
        return pltpu.make_async_remote_copy(
            ytx.at[k, d], yrx.at[k, d], y_send.at[k, d], y_recv.at[k, d],
            device_id={"gy": to}, device_id_type=MESH,
        )

    def finish(k):
        t, c = order[k]
        out_ref[t, c] = yown[k].reshape(cx, cy, nz)
        for d, receives in ((0, low), (1, high)):

            @pl.when(receives)
            def _(d=d):
                y_copy(k, d, gy).wait_recv()
                out_ref[t, c] += yrx[k, d].astype(jnp.float32).reshape(cx, cy, nz)

    for k in range(len(order)):
        acc = own[k]
        if n_gx <= 4:
            for s in range(1, n_gx):
                acc = acc + receive(k, s)
        else:

            acc = lax.fori_loop(1, n_gx, lambda s, acc, k=k: acc + receive(k, s), acc)
        hi, lo = halves(acc)
        wide = jnp.dot(
            jnp.concatenate([hi, lo], axis=0), tmat[...], preferred_element_type=jnp.float32
        )
        zs = 0.5 * acc + (wide[:cells] + wide[cells:]) * inv
        hi, lo = halves(zs)
        v = jnp.dot(
            ymats, jnp.concatenate([hi, lo, hi], axis=0), preferred_element_type=jnp.float32
        )
        yown[k] = v[:cells]
        ytx[k, 0] = v[cells : 2 * cells].astype(jnp.bfloat16)
        ytx[k, 1] = v[2 * cells :].astype(jnp.bfloat16)
        pl.when(high)(y_copy(k, 0, gy + 1).start)
        pl.when(low)(y_copy(k, 1, gy - 1).start)
        if k > 0:
            finish(k - 1)
    finish(len(order) - 1)

    for sends, _, copy, _, _ in exchanges:
        pl.when(sends)(copy.wait_send)
    for k in range(len(order)):
        each(1, n_gx, lambda s, k=k: settle(k, s))
        pl.when(high)(y_copy(k, 0, gy).wait_send)
        pl.when(low)(y_copy(k, 1, gy).wait_send)


def shards(velocity, moved_image, residual_weight, mark_values, mark_brick, mark_cell, band_widths):
    n_gx, n_gy = lax.axis_size("gx"), lax.axis_size("gy")
    steps, cx, cy, nz = moved_image.shape
    rows = mark_values.shape[0]
    cells = cx * cy
    chunks = 3 * steps
    lines = 2 * cells + rows // steps
    f32, bf16 = jnp.float32, jnp.bfloat16
    dma = pltpu.SemaphoreType.DMA
    vmem = pl.BlockSpec(memory_space=pltpu.VMEM)
    smoothed = pl.pallas_call(
        functools.partial(kernel, n_gx, n_gy, (steps, cx, cy, nz, rows)),
        out_shape=jax.ShapeDtypeStruct(velocity.shape, f32),
        in_specs=[pl.BlockSpec(memory_space=pltpu.SMEM)] + [vmem] * 5,
        out_specs=vmem,
        scratch_shapes=[
            pltpu.VMEM((chunks, n_gx, cells, nz), jnp.int16),
            pltpu.VMEM((chunks, n_gx, 1, nz), f32),
            pltpu.VMEM((chunks, cells, nz), f32),
            pltpu.VMEM((chunks, n_gx, cells, nz), jnp.int16),
            pltpu.VMEM((chunks, n_gx, 1, nz), f32),
            pltpu.VMEM((chunks, 2, cells, nz), bf16),
            pltpu.VMEM((chunks, cells, nz), f32),
            pltpu.VMEM((chunks, 2, cells, nz), bf16),
            pltpu.VMEM((2, steps, cy, nz), f32),
            pltpu.VMEM((2, steps * cx, nz), f32),
            pltpu.VMEM((2, steps * cx, nz), f32),
            pltpu.VMEM((steps, n_gx * cells, 2 * lines), bf16),
            pltpu.VMEM((nz, nz), bf16),
            dma((chunks, n_gx)),
            dma((chunks, n_gx)),
            dma((chunks, n_gx)),
            dma((chunks, n_gx)),
            dma((chunks, 2)),
            dma((chunks, 2)),
            dma((2,)),
            dma((2,)),
            dma((2,)),
            dma((2,)),
        ],
        compiler_params=pltpu.CompilerParams(
            collective_id=0, has_side_effects=True, vmem_limit_bytes=40 * 2**20
        ),
        cost_estimate=pl.CostEstimate(
            flops=4 * 10**8, bytes_accessed=2 * 10**6, transcendentals=0
        ),
    )(
        band_widths,
        moved_image,
        residual_weight,
        mark_values.transpose(1, 0, 2),
        mark_brick.reshape(1, rows),
        mark_cell.reshape(1, rows),
    )
    return velocity - smoothed


def solution(mesh):
    return jax.shard_map(
        shards,
        mesh=mesh,
        in_specs=(
            P(("group", "ta"), None, "gx", "gy", None),
            P(("group", "ta"), "gx", "gy", None),
            P(("group", "ta"), "gx", "gy", None),
            P(("group", "gx", "gy", "ta"), None, None),
            P(("group", "gx", "gy", "ta"), None),
            P(("group", "gx", "gy", "ta"), None),
            P(),
        ),
        out_specs=P(("group", "ta"), None, "gx", "gy", None),
        check_vma=False,
    )
```

time: 125 us -> 34.9 us (0.28)
  starting transfers between devices: 33.5 us -> 0 us
  Pallas kernels: 0 us -> 30.4 us
  local copies, waits for them, and re-layouts: 33.8 us -> 3.49 us
  waiting for transfers between devices: 28.9 us -> 0 us
  blocking collectives: 13.6 us -> 0 us
  matrix products: 6.99 us -> 0 us
  other arithmetic: 5.27 us -> 0.81 us
  between operations: 2.04 us -> 0.02 us
    pallas_call x0 -> x1, Pallas kernels: none -> 30.4 us  [shards(): pl.pallas_call(functools.partial(kernel, n_gx, n_gy, (steps, cx, cy, nz,...]
    all_to_all x3 -> x0, starting transfers between devices: 18.9 us -> none  [the longest x1 9.13 us: shards(): lax.all_to_all(total, 'gx', split_axis=4, concat_axis=2, tiled=True)]
    ppermute x6 -> x0, waiting for transfers between devices: 18.2 us -> none  [the longest x3 10.9 us: extended(): before = lax.ppermute(last, axis, up)]
    unnamed x12 -> x14, local copies, waits for them, and re-layouts: 21.3 us -> 3.49 us
    ppermute x6 -> x0, starting transfers between devices: 14.5 us -> none  [the longest x3 10.7 us: extended(): before = lax.ppermute(last, axis, up)]
    all_to_all x1 -> x0, blocking collectives: 13.6 us -> none  [shards(): lax.all_to_all(result.reshape(arrived.shape), 'gx', split_axis=2, concat_...]
    all_to_all x3 -> x0, waiting for transfers between devices: 10.8 us -> none  [the longest x1 7.87 us: shards(): lax.all_to_all(total, 'gx', split_axis=4, concat_axis=2, tiled=True)]
    dot_general x5 -> x0, matrix products: 6.99 us -> none  [the longest x1 2.83 us: shards(): jnp.einsum('tcxyj,ij->tcxyi', along_second, square_matrix(cells_z, band_w...]
  transfers between devices with their start and end apart: 9 -> 0, of which waited for: 6 -> 0; matrix products, arithmetic and copies ran while one was open for 4% -> 0% of each run, Pallas kernels for 0% -> 0%
where the time goes in v1:
time: 34.9 us; the launch traced here: 34.8 us
  Pallas kernels  30.4 us (87%)
  local copies, waits for them, and re-layouts  3.49 us (10%)
  other arithmetic  0.81 us (2%)
    pallas_call x1, Pallas kernels, shards(): pl.pallas_call(functools.partial(kernel, n_gx, n_gy, (steps, cx, cy, nz,...  30.4 us
    unnamed x14, local copies, waits for them, and re-layouts  3.49 us
    sub x1, other arithmetic, shards(): return velocity - smoothed  0.81 us

profile of v1, /device:TPU:0, one launch (start us, length us, event | category | flops | bytes accessed | tf_op | source)
XLA Modules:
  0.0 34.8 jit_solution(15281301448091155699)
XLA Ops:
  0.0 0.0 copy-start.3
  0.0 0.0 copy-start.4
  0.0 0.0 copy-start.5
  0.0 0.6 %copy-done.3 = s32[3]{0:T(128)S(1)} copy-done((s32[3]{0:T(128)S(1)}, s32[3]{0:T(128)}, u32[]{:S(2)}) %copy-start.3) | copy-done | bytes 36
  0.7 0.0 copy-done.4
  0.7 0.0 copy-done.5
  0.7 0.0 copy-start
  0.7 1.0 %copy-done = bf16[128,3,512]{2,0,1:T(8,128)(2,1)S(1)} copy-done((bf16[128,3,512]{2,0,1:T(8,128)(2,1)S(1)}, bf16[128,3,512]{2,0,1:T(8,128)(2,1)}, u32[]{:S(2)}) %copy-start) | copy-done | bytes 393240
  1.7 0.0 copy-start.1
  1.7 0.9 %copy-done.1 = f32[2,4,8,512]{3,2,1,0:T(8,128)S(1)} copy-done((f32[2,4,8,512]{3,2,1,0:T(8,128)S(1)}, f32[2,4,8,512]{3,2,1,0:T(8,128)}, u32[]{:S(2)}) %copy-start.1) | copy-done | bytes 131096
  2.6 0.0 copy-start.2
  2.6 0.9 %copy-done.2 = f32[2,4,8,512]{3,2,1,0:T(8,128)S(1)} copy-done((f32[2,4,8,512]{3,2,1,0:T(8,128)S(1)}, f32[2,4,8,512]{3,2,1,0:T(8,128)}, u32[]{:S(2)}) %copy-start.2) | copy-done | bytes 131096
  3.5 0.0 copy-start.6
  3.5 30.4 %shard_map.73 = f32[2,3,4,8,512]{4,3,2,1,0:T(8,128)S(1)} custom-call(s32[3]{0:T(128)S(1)} %copy-done.3, f32[2,4,8,512]{3,2,1,0:T(8,128)S(1)} %copy-done.1, f32[2,4,8,512]{3,2,1,0:T(8,128)S(1)} %copy-done.2, bf16[3,128,512]{2,1,0:T(8,128)(2,1)S(1)} %bitcast.3, s32[1,128]{1,0:T(1,128)S(1)} %bitcast.4, s32[1,128]{1,0:T(1,128)S(1)} %bitcast.5), custom_call_target="tpu_custom_call" | custom-call | flops 400000000 | bytes 2000000 | tf_op jit(solution)/shard_map/pallas_call | solution.py:275
  33.9 0.0 copy-done.6
  34.0 0.8 %sub.3 = f32[2,3,4,8,512]{4,3,2,1,0:T(8,128)} subtract(f32[2,3,4,8,512]{4,3,2,1,0:T(8,128)S(1)} %copy-done.6, f32[2,3,4,8,512]{4,3,2,1,0:T(8,128)S(1)} %shard_map.73) | non-fusion elementwise | flops 98304 | bytes 1179648 | tf_op jit(solution)/shard_map/sub | solution.py:319
Async XLA Ops:
  0.0 0.7 %copy-start.3 = (s32[3]{0:T(128)S(1)}, s32[3]{0:T(128)}, u32[]{:S(2)}) copy-start(s32[3]{0:T(128)} %width_ref.1) | copy-start | bytes 40
  0.0 0.7 %copy-start.4 = (s32[128,1]{0,1:T(1,128)S(1)}, s32[128,1]{0,1:T(1,128)}, u32[]{:S(2)}) copy-start(s32[128,1]{0,1:T(1,128)} %param.11) | copy-start | bytes 1540
  0.0 0.7 %copy-start.5 = (s32[128,1]{0,1:T(1,128)S(1)}, s32[128,1]{0,1:T(1,128)}, u32[]{:S(2)}) copy-start(s32[128,1]{0,1:T(1,128)} %param.12) | copy-start | bytes 1540
  0.7 1.0 %copy-start = (bf16[128,3,512]{2,0,1:T(8,128)(2,1)S(1)}, bf16[128,3,512]{2,0,1:T(8,128)(2,1)}, u32[]{:S(2)}) copy-start(bf16[128,3,512]{2,0,1:T(8,128)(2,1)} %param.10) | copy-start | bytes 1179652
  1.7 0.9 %copy-start.1 = (f32[2,4,8,512]{3,2,1,0:T(8,128)S(1)}, f32[2,4,8,512]{3,2,1,0:T(8,128)}, u32[]{:S(2)}) copy-start(f32[2,4,8,512]{3,2,1,0:T(8,128)} %image_ref.1) | copy-start | bytes 393220
  2.6 0.9 %copy-start.2 = (f32[2,4,8,512]{3,2,1,0:T(8,128)S(1)}, f32[2,4,8,512]{3,2,1,0:T(8,128)}, u32[]{:S(2)}) copy-start(f32[2,4,8,512]{3,2,1,0:T(8,128)} %weight_ref.1) | copy-start | bytes 393220
  3.5 30.4 %copy-start.6 = (f32[2,3,4,8,512]{4,3,2,1,0:T(8,128)S(1)}, f32[2,3,4,8,512]{4,3,2,1,0:T(8,128)}, u32[]{:S(2)}) copy-start(f32[2,3,4,8,512]{4,3,2,1,0:T(8,128)} %param.7) | copy-start | bytes 1179652

commit v2 on v1

--- a/solution.py
+++ b/solution.py
@@ -33,7 +33,8 @@
 
 
 def kernel(
-    n_gx, n_gy, dims, width_ref, image_ref, weight_ref, mark_ref, brick_ref, cell_ref, out_ref,
+    n_gx, n_gy, dims, width_hbm, image_hbm, weight_hbm, mark_hbm, brick_hbm, cell_hbm, out_hbm,
+    width_ref, image_ref, weight_ref, mark_ref, brick_ref, cell_ref, out_ref, load_sem, store_sem,
     tx, scale_out, own, rx, scale_in, ytx, yown, yrx, edge_x, edge_y_out, edge_y, kmat, tmat,
     tx_send, rx_recv, s_send, s_recv, y_send, y_recv, ex_send, ex_recv, ey_send, ey_recv,
 ):
@@ -46,6 +47,17 @@
     low, high = gy > 0, gy < n_gy - 1
     barrier = pltpu.get_barrier_semaphore()
 
+    names = ("width", "brick", "cell", "image", "weight", "mark0", "mark1", "mark2")
+    pairs = [(width_hbm, width_ref), (brick_hbm, brick_ref), (cell_hbm, cell_ref)]
+    pairs += [(image_hbm, image_ref), (weight_hbm, weight_ref)]
+    pairs += [(mark_hbm.at[c], mark_ref.at[c]) for c in range(3)]
+    loads = {
+        name: pltpu.make_async_copy(src, dst, load_sem.at[i])
+        for i, (name, (src, dst)) in enumerate(zip(names, pairs))
+    }
+    for name in ("image", "width", "brick", "cell", "weight", "mark2", "mark0", "mark1"):
+        loads[name].start()
+
     def greet(s):
         pl.semaphore_signal(
             barrier, inc=1, device_id={"gx": lax.rem(gx + s, n_gx)}, device_id_type=MESH
@@ -61,12 +73,42 @@
     def _():
         pl.semaphore_signal(barrier, inc=1, device_id={"gy": gy + 1}, device_id_type=MESH)
 
+    loads["image"].wait()
     for t in range(steps):
         for x in range(cx):
             r = t * cx + x
             edge_y_out[0, r : r + 1, :] = image_ref[t, x, 0:1, :]
             edge_y_out[1, r : r + 1, :] = image_ref[t, x, cy - 1 : cy, :]
 
+    pl.semaphore_wait(barrier, n_gx - 1 + low.astype(jnp.int32) + high.astype(jnp.int32))
+
+    def x_edge(d, plane, to):
+        return pltpu.make_async_remote_copy(
+            image_ref.at[:, plane], edge_x.at[d], ex_send.at[d], ex_recv.at[d],
+            device_id={"gx": to}, device_id_type=MESH,
+        )
+
+    def y_edge(d, side, to):
+        return pltpu.make_async_remote_copy(
+            edge_y_out.at[side], edge_y.at[d], ey_send.at[d], ey_recv.at[d],
+            device_id={"gy": to}, device_id_type=MESH,
+        )
+
+    exchanges = (
+        (right, left, x_edge(0, cx - 1, gx + 1), edge_x, 0),
+        (left, right, x_edge(1, 0, gx - 1), edge_x, 1),
+        (high, low, y_edge(0, 1, gy + 1), edge_y, 0),
+        (low, high, y_edge(1, 0, gy - 1), edge_y, 1),
+    )
+    for sends, receives, copy, buffer, d in exchanges:
+        pl.when(sends)(copy.start)
+
+        @pl.when(jnp.logical_not(receives))
+        def _(buffer=buffer, d=d):
+            buffer[d] = jnp.zeros(buffer.shape[1:], buffer.dtype)
+
+    for name in ("width", "brick", "cell"):
+        loads[name].wait()
     group = math.gcd(n_gx, 4)
     block = group * cells
     lane = lax.broadcasted_iota(jnp.int32, (1, lines), 1)
@@ -89,33 +131,6 @@
 
         each(0, n_gx // group, build)
 
-    pl.semaphore_wait(barrier, n_gx - 1 + low.astype(jnp.int32) + high.astype(jnp.int32))
-
-    def x_edge(d, plane, to):
-        return pltpu.make_async_remote_copy(
-            image_ref.at[:, plane], edge_x.at[d], ex_send.at[d], ex_recv.at[d],
-            device_id={"gx": to}, device_id_type=MESH,
-        )
-
-    def y_edge(d, side, to):
-        return pltpu.make_async_remote_copy(
-            edge_y_out.at[side], edge_y.at[d], ey_send.at[d], ey_recv.at[d],
-            device_id={"gy": to}, device_id_type=MESH,
-        )
-
-    exchanges = (
-        (right, left, x_edge(0, cx - 1, gx + 1), edge_x, 0),
-        (left, right, x_edge(1, 0, gx - 1), edge_x, 1),
-        (high, low, y_edge(0, 1, gy + 1), edge_y, 0),
-        (low, high, y_edge(1, 0, gy - 1), edge_y, 1),
-    )
-    for sends, receives, copy, buffer, d in exchanges:
-        pl.when(sends)(copy.start)
-
-        @pl.when(jnp.logical_not(receives))
-        def _(buffer=buffer, d=d):
-            buffer[d] = jnp.zeros(buffer.shape[1:], buffer.dtype)
-
     def brick_copy(k, s):
         return pltpu.make_async_remote_copy(
             tx.at[k, s], rx.at[k, s], tx_send.at[k, s], rx_recv.at[k, s],
@@ -146,6 +161,10 @@
         if k == steps:
             for _, receives, copy, _, _ in exchanges:
                 pl.when(receives)(copy.wait_recv)
+        if k == 0:
+            loads["weight"].wait()
+        if t == 0:
+            loads[names[5 + c]].wait()
         m = image_ref[t]
         if c == 2:
             flat = m.reshape(cells, nz)
@@ -218,6 +237,10 @@
             device_id={"gy": to}, device_id_type=MESH,
         )
 
+    def store(k):
+        t, c = order[k]
+        return pltpu.make_async_copy(out_ref.at[t, c], out_hbm.at[t, c], store_sem.at[k])
+
     def finish(k):
         t, c = order[k]
         out_ref[t, c] = yown[k].reshape(cx, cy, nz)
@@ -227,6 +250,8 @@
             def _(d=d):
                 y_copy(k, d, gy).wait_recv()
                 out_ref[t, c] += yrx[k, d].astype(jnp.float32).reshape(cx, cy, nz)
+
+        store(k).start()
 
     for k in range(len(order)):
         acc = own[k]
@@ -260,6 +285,7 @@
         each(1, n_gx, lambda s, k=k: settle(k, s))
         pl.when(high)(y_copy(k, 0, gy).wait_send)
         pl.when(low)(y_copy(k, 1, gy).wait_send)
+        store(k).wait()
 
 
 def shards(velocity, moved_image, residual_weight, mark_values, mark_brick, mark_cell, band_widths):
@@ -271,13 +297,21 @@
     lines = 2 * cells + rows // steps
     f32, bf16 = jnp.float32, jnp.bfloat16
     dma = pltpu.SemaphoreType.DMA
-    vmem = pl.BlockSpec(memory_space=pltpu.VMEM)
     smoothed = pl.pallas_call(
         functools.partial(kernel, n_gx, n_gy, (steps, cx, cy, nz, rows)),
         out_shape=jax.ShapeDtypeStruct(velocity.shape, f32),
-        in_specs=[pl.BlockSpec(memory_space=pltpu.SMEM)] + [vmem] * 5,
-        out_specs=vmem,
+        in_specs=[pl.BlockSpec(memory_space=pltpu.HBM)] * 6,
+        out_specs=pl.BlockSpec(memory_space=pltpu.HBM),
         scratch_shapes=[
+            pltpu.SMEM(band_widths.shape, jnp.int32),
+            pltpu.VMEM(moved_image.shape, f32),
+            pltpu.VMEM(residual_weight.shape, f32),
+            pltpu.VMEM((3, rows, nz), bf16),
+            pltpu.VMEM((1, rows), jnp.int32),
+            pltpu.VMEM((1, rows), jnp.int32),
+            pltpu.VMEM(velocity.shape, f32),
+            dma((8,)),
+            dma((chunks,)),
             pltpu.VMEM((chunks, n_gx, cells, nz), jnp.int16),
             pltpu.VMEM((chunks, n_gx, 1, nz), f32),
             pltpu.VMEM((chunks, cells, nz), f32),
@@ -303,7 +337,7 @@
             dma((2,)),
         ],
         compiler_params=pltpu.CompilerParams(
-            collective_id=0, has_side_effects=True, vmem_limit_bytes=40 * 2**20
+            collective_id=0, has_side_effects=True, vmem_limit_bytes=63 * 2**20
         ),
         cost_estimate=pl.CostEstimate(
             flops=4 * 10**8, bytes_accessed=2 * 10**6, transcendentals=0

time: 34.9 us -> 32.5 us (0.931)
  local copies, waits for them, and re-layouts: 3.49 us -> 0.01 us
  other arithmetic: 0.81 us -> 1.8 us
    unnamed x14 -> x2, local copies, waits for them, and re-layouts: 3.49 us -> 0.01 us
    sub x1, other arithmetic: 0.81 us -> 1.8 us  [shards(): return velocity - smoothed]
where the time goes in v2:
time: 32.5 us; the launch traced here: 32.3 us
  Pallas kernels  30.5 us (94%)
  other arithmetic  1.8 us (6%)
    pallas_call x1, Pallas kernels, shards(): pl.pallas_call(functools.partial(kernel, n_gx, n_gy, (steps, cx, cy, nz,...  30.5 us
    sub x1, other arithmetic, shards(): return velocity - smoothed  1.8 us

profile of v2, /device:TPU:0, one launch (start us, length us, event | category | flops | bytes accessed | tf_op | source)
XLA Modules:
  0.0 32.3 jit_solution(16158278784100871200)
XLA Ops:
  0.0 0.0 copy-start
  0.0 30.5 %shard_map.73 = f32[2,3,4,8,512]{4,3,2,1,0:T(8,128)} custom-call(s32[3]{0:T(128)} %width_hbm.1, f32[2,4,8,512]{3,2,1,0:T(8,128)} %image_hbm.1, f32[2,4,8,512]{3,2,1,0:T(8,128)} %weight_hbm.1, bf16[3,128,512]{2,1,0:T(8,128)(2,1)} %bitcast.3, s32[1,128]{1,0:T(1,128)} %bitcast.4, s32[1,128]{1,0:T(1,128)} %bitcast.5), custom_call_target="tpu_custom_call" | custom-call | flops 400000000 | bytes 2000000 | tf_op jit(solution)/shard_map/pallas_call | solution.py:300
  30.5 0.0 copy-done
  30.5 1.8 %sub.3 = f32[2,3,4,8,512]{4,3,2,1,0:T(8,128)} subtract(f32[2,3,4,8,512]{4,3,2,1,0:T(8,128)S(1)} %copy-done, f32[2,3,4,8,512]{4,3,2,1,0:T(8,128)} %shard_map.73) | non-fusion elementwise | flops 98304 | bytes 1179648 | tf_op jit(solution)/shard_map/sub | solution.py:353
Async XLA Ops:
  0.0 30.5 %copy-start = (f32[2,3,4,8,512]{4,3,2,1,0:T(8,128)S(1)}, f32[2,3,4,8,512]{4,3,2,1,0:T(8,128)}, u32[]{:S(2)}) copy-start(f32[2,3,4,8,512]{4,3,2,1,0:T(8,128)} %param.7) | copy-start | bytes 1179652

commit v3 on v2

--- a/solution.py
+++ b/solution.py
@@ -9,6 +9,7 @@
 from jax.sharding import PartitionSpec as P
 
 LEVELS = 32000.0
+LAG = 2
 MESH = pl.DeviceIdType.MESH
 
 
@@ -73,15 +74,6 @@
     def _():
         pl.semaphore_signal(barrier, inc=1, device_id={"gy": gy + 1}, device_id_type=MESH)
 
-    loads["image"].wait()
-    for t in range(steps):
-        for x in range(cx):
-            r = t * cx + x
-            edge_y_out[0, r : r + 1, :] = image_ref[t, x, 0:1, :]
-            edge_y_out[1, r : r + 1, :] = image_ref[t, x, cy - 1 : cy, :]
-
-    pl.semaphore_wait(barrier, n_gx - 1 + low.astype(jnp.int32) + high.astype(jnp.int32))
-
     def x_edge(d, plane, to):
         return pltpu.make_async_remote_copy(
             image_ref.at[:, plane], edge_x.at[d], ex_send.at[d], ex_recv.at[d],
@@ -100,13 +92,6 @@
         (high, low, y_edge(0, 1, gy + 1), edge_y, 0),
         (low, high, y_edge(1, 0, gy - 1), edge_y, 1),
     )
-    for sends, receives, copy, buffer, d in exchanges:
-        pl.when(sends)(copy.start)
-
-        @pl.when(jnp.logical_not(receives))
-        def _(buffer=buffer, d=d):
-            buffer[d] = jnp.zeros(buffer.shape[1:], buffer.dtype)
-
     for name in ("width", "brick", "cell"):
         loads[name].wait()
     group = math.gcd(n_gx, 4)
@@ -131,6 +116,13 @@
 
         each(0, n_gx // group, build)
 
+    loads["image"].wait()
+    for t in range(steps):
+        for x in range(cx):
+            r = t * cx + x
+            edge_y_out[0, r : r + 1, :] = image_ref[t, x, 0:1, :]
+            edge_y_out[1, r : r + 1, :] = image_ref[t, x, cy - 1 : cy, :]
+
     def brick_copy(k, s):
         return pltpu.make_async_remote_copy(
             tx.at[k, s], rx.at[k, s], tx_send.at[k, s], rx_recv.at[k, s],
@@ -155,6 +147,16 @@
     def settle(k, s):
         brick_copy(k, s).wait_send()
         scale_copy(k, s).wait_send()
+
+    def meet():
+        pl.semaphore_wait(barrier, n_gx - 1 + low.astype(jnp.int32) + high.astype(jnp.int32))
+
+        for sends, receives, copy, buffer, d in exchanges:
+            pl.when(sends)(copy.start)
+
+            @pl.when(jnp.logical_not(receives))
+            def _(buffer=buffer, d=d):
+                buffer[d] = jnp.zeros(buffer.shape[1:], buffer.dtype)
 
     order = [(t, c) for c in (2, 0, 1) for t in range(steps)]
     for k, (t, c) in enumerate(order):
@@ -212,7 +214,10 @@
                             own[k] = piece
 
         each(0, n_gx // group, spread)
-        each(1, n_gx, lambda s, k=k: send(k, s))
+        if k == steps - 1:
+            meet()
+        for ready in range(steps) if k == steps - 1 else [k] if k >= steps else []:
+            each(1, n_gx, lambda s, k=ready: send(k, s))
 
     zi = lax.broadcasted_iota(jnp.int32, (nz, nz), 0)
     zj = lax.broadcasted_iota(jnp.int32, (nz, nz), 1)
@@ -275,9 +280,10 @@
         ytx[k, 1] = v[2 * cells :].astype(jnp.bfloat16)
         pl.when(high)(y_copy(k, 0, gy + 1).start)
         pl.when(low)(y_copy(k, 1, gy - 1).start)
-        if k > 0:
-            finish(k - 1)
-    finish(len(order) - 1)
+        if k >= LAG:
+            finish(k - LAG)
+    for k in range(len(order) - LAG, len(order)):
+        finish(k)
 
     for sends, _, copy, _, _ in exchanges:
         pl.when(sends)(copy.wait_send)

time: 32.5 us -> 32.1 us (0.988)
  Pallas kernels: 30.5 us -> 30.1 us
    pallas_call x1, Pallas kernels: 30.5 us -> 30.1 us  [shards(): pl.pallas_call(functools.partial(kernel, n_gx, n_gy, (steps, cx, cy, nz,...]
where the time goes in v3:
time: 32.1 us; the launch traced here: 31.9 us
  Pallas kernels  30.1 us (94%)
  other arithmetic  1.8 us (6%)
    pallas_call x1, Pallas kernels, shards(): pl.pallas_call(functools.partial(kernel, n_gx, n_gy, (steps, cx, cy, nz,...  30.1 us
    sub x1, other arithmetic, shards(): return velocity - smoothed  1.8 us

profile of v3, /device:TPU:0, one launch (start us, length us, event | category | flops | bytes accessed | tf_op | source)
XLA Modules:
  0.0 31.9 jit_solution(16123683410462194080)
XLA Ops:
  0.0 0.0 copy-start
  0.0 30.1 %shard_map.73 = f32[2,3,4,8,512]{4,3,2,1,0:T(8,128)} custom-call(s32[3]{0:T(128)} %width_hbm.1, f32[2,4,8,512]{3,2,1,0:T(8,128)} %image_hbm.1, f32[2,4,8,512]{3,2,1,0:T(8,128)} %weight_hbm.1, bf16[3,128,512]{2,1,0:T(8,128)(2,1)} %bitcast.3, s32[1,128]{1,0:T(1,128)} %bitcast.4, s32[1,128]{1,0:T(1,128)} %bitcast.5), custom_call_target="tpu_custom_call" | custom-call | flops 400000000 | bytes 2000000 | tf_op jit(solution)/shard_map/pallas_call | solution.py:306
  30.1 0.0 copy-done
  30.1 1.8 %sub.3 = f32[2,3,4,8,512]{4,3,2,1,0:T(8,128)} subtract(f32[2,3,4,8,512]{4,3,2,1,0:T(8,128)S(1)} %copy-done, f32[2,3,4,8,512]{4,3,2,1,0:T(8,128)} %shard_map.73) | non-fusion elementwise | flops 98304 | bytes 1179648 | tf_op jit(solution)/shard_map/sub | solution.py:359
Async XLA Ops:
  0.0 30.1 %copy-start = (f32[2,3,4,8,512]{4,3,2,1,0:T(8,128)S(1)}, f32[2,3,4,8,512]{4,3,2,1,0:T(8,128)}, u32[]{:S(2)}) copy-start(f32[2,3,4,8,512]{4,3,2,1,0:T(8,128)} %param.7) | copy-start | bytes 1179652

commit v4 on v3

--- a/solution.py
+++ b/solution.py
@@ -142,7 +142,9 @@
     def receive(k, s):
         brick_copy(k, s).wait_recv()
         scale_copy(k, s).wait_recv()
-        return rx[k, s].astype(jnp.int32).astype(jnp.float32) * scale_in[k, s]
+        return rx[k, s].astype(jnp.int32).astype(jnp.float32) * jnp.concatenate(
+            [scale_in[k, s]] * (nz // 128), axis=1
+        )
 
     def settle(k, s):
         brick_copy(k, s).wait_send()
@@ -202,7 +204,9 @@
                 piece = p[i * cells : (i + 1) * cells]
                 s = g * group + i
                 top = jnp.maximum(jnp.max(jnp.abs(piece), axis=0, keepdims=True), 1e-30)
-                tx[k, s] = jnp.round(piece * (LEVELS / top)).astype(jnp.int32).astype(jnp.int16)
+                top = functools.reduce(jnp.maximum, [top[:, z : z + 128] for z in range(0, nz, 128)])
+                fit = jnp.concatenate([LEVELS / top] * (nz // 128), axis=1)
+                tx[k, s] = jnp.round(piece * fit).astype(jnp.int32).astype(jnp.int16)
                 scale_out[k, s] = top * (1.0 / LEVELS)
                 if i == 0:
                     if n_gx == group:
@@ -319,10 +323,10 @@
             dma((8,)),
             dma((chunks,)),
             pltpu.VMEM((chunks, n_gx, cells, nz), jnp.int16),
-            pltpu.VMEM((chunks, n_gx, 1, nz), f32),
+            pltpu.VMEM((chunks, n_gx, 1, 128), f32),
             pltpu.VMEM((chunks, cells, nz), f32),
             pltpu.VMEM((chunks, n_gx, cells, nz), jnp.int16),
-            pltpu.VMEM((chunks, n_gx, 1, nz), f32),
+            pltpu.VMEM((chunks, n_gx, 1, 128), f32),
             pltpu.VMEM((chunks, 2, cells, nz), bf16),
             pltpu.VMEM((chunks, cells, nz), f32),
             pltpu.VMEM((chunks, 2, cells, nz), bf16),

time: 32.1 us -> 31.4 us (0.978)
  Pallas kernels: 30.1 us -> 29.4 us
    pallas_call x1, Pallas kernels: 30.1 us -> 29.4 us  [shards(): pl.pallas_call(functools.partial(kernel, n_gx, n_gy, (steps, cx, cy, nz,...]
where the time goes in v4:
time: 31.4 us; the launch traced here: 31.2 us
  Pallas kernels  29.4 us (94%)
  other arithmetic  1.8 us (6%)
    pallas_call x1, Pallas kernels, shards(): pl.pallas_call(functools.partial(kernel, n_gx, n_gy, (steps, cx, cy, nz,...  29.4 us
    sub x1, other arithmetic, shards(): return velocity - smoothed  1.8 us

profile of v4, /device:TPU:0, one launch (start us, length us, event | category | flops | bytes accessed | tf_op | source)
XLA Modules:
  0.0 31.2 jit_solution(6118114665670144680)
XLA Ops:
  0.0 0.0 copy-start
  0.0 29.4 %shard_map.73 = f32[2,3,4,8,512]{4,3,2,1,0:T(8,128)} custom-call(s32[3]{0:T(128)} %width_hbm.1, f32[2,4,8,512]{3,2,1,0:T(8,128)} %image_hbm.1, f32[2,4,8,512]{3,2,1,0:T(8,128)} %weight_hbm.1, bf16[3,128,512]{2,1,0:T(8,128)(2,1)} %bitcast.3, s32[1,128]{1,0:T(1,128)} %bitcast.4, s32[1,128]{1,0:T(1,128)} %bitcast.5), custom_call_target="tpu_custom_call" | custom-call | flops 400000000 | bytes 2000000 | tf_op jit(solution)/shard_map/pallas_call | solution.py:310
  29.4 0.0 copy-done
  29.4 1.8 %sub.3 = f32[2,3,4,8,512]{4,3,2,1,0:T(8,128)} subtract(f32[2,3,4,8,512]{4,3,2,1,0:T(8,128)S(1)} %copy-done, f32[2,3,4,8,512]{4,3,2,1,0:T(8,128)} %shard_map.73) | non-fusion elementwise | flops 98304 | bytes 1179648 | tf_op jit(solution)/shard_map/sub | solution.py:363
Async XLA Ops:
  0.0 29.4 %copy-start = (f32[2,3,4,8,512]{4,3,2,1,0:T(8,128)S(1)}, f32[2,3,4,8,512]{4,3,2,1,0:T(8,128)}, u32[]{:S(2)}) copy-start(f32[2,3,4,8,512]{4,3,2,1,0:T(8,128)} %param.7) | copy-start | bytes 1179652
